TPU v7x, 256 devices: a whole 4x4x8 slice. The times are simulated.
256 devices in a mesh: dp: 16 (over z, core), cent: 16 (over x, y).
Axes of the slice: x: 4, y: 4, z: 8, core: 2. Of those that a mesh axis runs over, the one named last changes fastest.
Arguments:
- embeds: bfloat16 [24576, 1024], P('dp'), as said below
- centroids: bfloat16 [16384, 1024], P('cent'), as said below
Outputs:
- new_centroids: bfloat16 [16384, 1024], P('cent')
- row_lse: float32 [24576], P('dp')
Inputs may be any that keep to these rules, and one draw needn't show every extreme that they name: `centroids`: centroids lie within -0.6 to 0.6. `embeds`: embeddings lie within -6 to 6.
All inputs are finite; a program needn't handle non-finite values.
Results may differ from a plain program's by a relative error of at most 0.012.
The roundings to bfloat16 on the way count: a program that leaves them out, or rounds other values in their place, can miss the bound.
Values may be sent and summed in bfloat16 or wider, within the bound.
A program may use at most 64 MiB of HBM per device.

v0:
```python
import jax
import jax.numpy as jnp
from jax import lax
from jax.sharding import PartitionSpec as P

ITERS = 2


inverse_temp = 2.5


def per_device(embeds, centroids):
    current = centroids
    last_lse = jnp.zeros((embeds.shape[0],), jnp.float32)
    for turn in range(ITERS):
        norms = jnp.sum(jnp.square(current.astype(jnp.float32)), axis=1)
        scores = inverse_temp * (
            jnp.dot(embeds, current.T, preferred_element_type=jnp.float32) - 0.5 * norms[None, :]
        )
        local_top = jnp.max(scores, axis=1)
        highest = lax.pmax(local_top, "cent")
        total = lax.psum(jnp.sum(jnp.exp(scores - highest[:, None]), axis=1), "cent")
        last_lse = highest + jnp.log(total)
        weights = jnp.exp(scores - last_lse[:, None]).astype(jnp.bfloat16)
        sums = lax.dot_general(
            weights, embeds, (((0,), (0,)), ((), ())), preferred_element_type=jnp.float32
        )
        mass = jnp.sum(weights.astype(jnp.float32), axis=0)
        owned, owned_mass = (
            lax.psum_scatter(sums, "dp", scatter_dimension=0, tiled=True),
            lax.psum_scatter(mass[:, None], "dp", scatter_dimension=0, tiled=True),
        )
        count = owned.shape[0]
        offset = lax.axis_index("dp") * count
        older = lax.dynamic_slice_in_dim(current, offset, count, 0).astype(jnp.float32)
        fresh = ((owned + older) / (owned_mass + 1.0)).astype(jnp.bfloat16)
        current = lax.all_gather(fresh, "dp", axis=0, tiled=True)
    return (current, last_lse)


def solution(mesh):
    return jax.shard_map(
        per_device,
        mesh=mesh,
        in_specs=(P("dp", None), P("cent", None)),
        out_specs=(P("cent", None), P("dp")),
        check_vma=False,
    )
```

profile of v0, /device:TPU:1, one launch (start us, length us, event | category | flops | bytes accessed | tf_op | source)
XLA Modules:
  0.0 526.2 jit_solution(762343493077709523)
XLA Ops:
  7.2 0.0 copy-start
  7.2 0.0 reduce-scatter.13.cloned.1.call-start
  7.2 2.2 multiply_reduce_fusion.1
  9.5 0.2 copy-done
  9.7 7.0 %fusion = (f32[1536]{0:T(1024)S(1)}, f32[1536,1024]{0,1:T(8,128)}) fusion(f32[1024]{0:T(1024)S(1)} %broadcast_multiply_fusion.1, bf16[1536,1024]{1,0:T(8,128)(2,1)S(1)} %copy-done, bf16[1024,1024]{1,0:T(8,128)(2,1)} %param.3), kind=kOutput, calls=%fused_computation.8 | convolution fusion | flops 3225942528 | bytes 11544576 | tf_op jit(solution)/shard_map/dot_general | solution.py:18
  16.7 34.7 %pmax.14 = f32[1536]{0:T(1024)S(1)} all-reduce(f32[1536]{0:T(1024)S(1)} %get-tuple-element.2), channel_id=1, replica_groups=mesh['dp'=16,'cent'=16] {'cent'}, use_global_device_ids=true, to_apply=%region_2.0 | all-reduce | flops 1536 | bytes 12288 | tf_op jit(solution)/shard_map/pmax | solution.py:21
  51.4 4.1 exponential_reduce_fusion.1
  55.5 29.0 %psum.14 = f32[1536]{0:T(1024)S(1)} all-reduce(f32[1536]{0:T(1024)S(1)} %exponential_reduce_fusion.1), channel_id=1, replica_groups=mesh['dp'=16,'cent'=16] {'cent'}, use_global_device_ids=true, to_apply=%region_4.0 | all-reduce | flops 1536 | bytes 12288 | tf_op jit(solution)/shard_map/psum | solution.py:22
  84.5 4.2 convert_reduce_fusion.1
  88.7 1.0 copy.4
  89.7 0.0 reduce-scatter.13.cloned.1.call-update
  89.8 0.0 reduce-scatter.9.cloned.1.call-start
  89.8 8.0 %fusion.2 = f32[1024,1024]{1,0:T(8,128)} fusion(bf16[1536,1024]{1,0:T(8,128)(2,1)S(1)} %copy-done, f32[1536,1024]{0,1:T(8,128)} %get-tuple-element.3, f32[1536]{0:T(1024)S(1)} %log_add_fusion.1, f32[1024]{0:T(1024)S(1)} %broadcast_multiply_fusion.1), kind=kOutput, calls=%fused_computation.20 | convolution fusion | flops 3227516928 | bytes 13641728 | tf_op jit(solution)/shard_map/dot_general | solution.py:25
  97.8 0.0 reduce-scatter.9.cloned.1.call-update
  97.8 0.0 all-gather.3.cloned.1.call-start
  97.9 59.1 %reduce-scatter.13.cloned.1.call-done = f32[64,1]{1,0:T(8,128)} async-done(((f32[1024,1]{1,0:T(8,128)}), f32[64,1]{1,0:T(8,128)}) %reduce-scatter.13.cloned.1.call-update) | async-done | bytes 272
  156.9 0.8 broadcast_add_fusion.1
  157.7 0.1 copy.8
  157.8 63.1 %reduce-scatter.9.cloned.1.call-done = f32[64,1024]{1,0:T(8,128)} async-done(((f32[1024,1024]{1,0:T(8,128)}), f32[64,1024]{1,0:T(8,128)}) %reduce-scatter.9.cloned.1.call-update) | async-done | bytes 262160 | tf_op jit(solution)/shard_map/reduce_scatter | solution.py:30
  220.8 1.7 divide_convert_fusion.1
  222.6 0.0 all-gather.3.cloned.1.call-update
  222.6 0.0 reduce-scatter.15.cloned.1.call-start
  222.6 42.4 %all-gather.3.cloned.1.call-done = bf16[1024,1024]{1,0:T(8,128)(2,1)} async-done(((bf16[64,1024]{1,0:T(8,128)(2,1)}), bf16[1024,1024]{1,0:T(8,128)(2,1)}) %all-gather.3.cloned.1.call-update) | async-done | bytes 2097168 | tf_op jit(solution)/shard_map/all_gather | solution.py:37
  265.1 2.1 multiply_reduce_fusion
  267.2 7.0 %fusion.1 = (f32[1536]{0:T(1024)S(1)}, f32[1024,1536]{1,0:T(8,128)}) fusion(f32[1024]{0:T(1024)S(1)} %broadcast_multiply_fusion, bf16[1024,1024]{1,0:T(8,128)(2,1)} %all-gather.3.cloned.1.call-done, bf16[1536,1024]{1,0:T(8,128)(2,1)S(1)} %copy-done), kind=kOutput, calls=%fused_computation.9 | convolution fusion | flops 3225942528 | bytes 11544576 | tf_op jit(solution)/shard_map/dot_general | solution.py:18
  274.2 33.7 %pmax.15 = f32[1536]{0:T(1024)S(1)} all-reduce(f32[1536]{0:T(1024)S(1)} %get-tuple-element.4), channel_id=1, replica_groups=mesh['dp'=16,'cent'=16] {'cent'}, use_global_device_ids=true, to_apply=%region_10.0 | all-reduce | flops 1536 | bytes 12288 | tf_op jit(solution)/shard_map/pmax | solution.py:21
  307.8 4.1 exponential_reduce_fusion
  311.9 29.5 %psum.15 = f32[1536]{0:T(1024)S(1)} all-reduce(f32[1536]{0:T(1024)S(1)} %exponential_reduce_fusion), channel_id=1, replica_groups=mesh['dp'=16,'cent'=16] {'cent'}, use_global_device_ids=true, to_apply=%region_12.0 | all-reduce | flops 1536 | bytes 12288 | tf_op jit(solution)/shard_map/psum | solution.py:22
  341.5 0.0 copy-start.1
  341.5 4.2 convert_reduce_fusion
  345.6 1.0 copy.6
  346.7 0.0 reduce-scatter.15.cloned.1.call-update
  346.7 0.0 reduce-scatter.11.cloned.1.call-start
  346.8 8.0 %fusion.3 = f32[1024,1024]{1,0:T(8,128)} fusion(bf16[1536,1024]{1,0:T(8,128)(2,1)S(1)} %copy-done, f32[1024,1536]{1,0:T(8,128)} %get-tuple-element.5, f32[1536]{0:T(1024)S(1)} %log_add_fusion, f32[1024]{0:T(1024)S(1)} %broadcast_multiply_fusion), kind=kOutput, calls=%fused_computation.21 | convolution fusion | flops 3227516928 | bytes 13641728 | tf_op jit(solution)/shard_map/dot_general | solution.py:25
  354.7 0.0 copy-done.1
  354.7 0.0 reduce-scatter.11.cloned.1.call-update
  354.7 0.0 all-gather.5.cloned.1.call-start
  354.8 54.1 %reduce-scatter.15.cloned.1.call-done = f32[64,1]{1,0:T(8,128)} async-done(((f32[1024,1]{1,0:T(8,128)}), f32[64,1]{1,0:T(8,128)}) %reduce-scatter.15.cloned.1.call-update) | async-done | bytes 272
  408.9 0.8 broadcast_add_fusion
  409.7 0.1 copy.9
  409.7 62.4 %reduce-scatter.11.cloned.1.call-done = f32[64,1024]{1,0:T(8,128)} async-done(((f32[1024,1024]{1,0:T(8,128)}), f32[64,1024]{1,0:T(8,128)}) %reduce-scatter.11.cloned.1.call-update) | async-done | bytes 262160 | tf_op jit(solution)/shard_map/reduce_scatter | solution.py:30
  472.1 1.7 divide_convert_fusion
  473.9 0.0 all-gather.5.cloned.1.call-update
  473.9 42.4 %all-gather.5.cloned.1.call-done = bf16[1024,1024]{1,0:T(8,128)(2,1)} async-done(((bf16[64,1024]{1,0:T(8,128)(2,1)}), bf16[1024,1024]{1,0:T(8,128)(2,1)}) %all-gather.5.cloned.1.call-update) | async-done | bytes 2097168 | tf_op jit(solution)/shard_map/all_gather | solution.py:37
  516.3 3.1 copy.11
  (4 shorter events, 0.0 us)
Async XLA Ops:
  7.2 2.5 copy-start
  7.2 149.8 %reduce-scatter.13.cloned.1.call-start = ((), (), s32[]{:S(2)}) async-start(), calls=%async_computation.8 | async-start | bytes 557056
  89.8 131.1 %reduce-scatter.9.cloned.1.call-start = ((), (), s32[]{:S(2)}) async-start(), calls=%async_computation.4 | async-start | bytes 4456448 | tf_op jit(solution)/shard_map/reduce_scatter | solution.py:30
  97.8 167.2 %all-gather.3.cloned.1.call-start = ((), (), s32[]{:S(2)}) async-start(), calls=%async_computation.5 | async-start | bytes 2228224 | tf_op jit(solution)/shard_map/all_gather | solution.py:37
  222.6 186.3 %reduce-scatter.15.cloned.1.call-start = ((), (), s32[]{:S(2)}) async-start(), calls=%async_computation.9 | async-start | bytes 557056
  341.5 13.2 %copy-start.1 = (f32[1536]{0:T(1024)}, f32[1536]{0:T(1024)S(1)}, u32[]{:S(2)}) copy-start(f32[1536]{0:T(1024)S(1)} %log_add_fusion) | copy-start | bytes 18436
  346.7 125.4 %reduce-scatter.11.cloned.1.call-start = ((), (), s32[]{:S(2)}) async-start(), calls=%async_computation.6 | async-start | bytes 4456448 | tf_op jit(solution)/shard_map/reduce_scatter | solution.py:30
  354.7 161.6 %all-gather.5.cloned.1.call-start = ((), (), s32[]{:S(2)}) async-start(), calls=%async_computation.7 | async-start | bytes 2228224 | tf_op jit(solution)/shard_map/all_gather | solution.py:37
Sparse Core Ops, SparseCore 0:
  89.9 66.9 reduce-scatter.12
  159.6 61.1 reduce-scatter.8
  223.4 41.6 all-gather.2
  346.8 62.0 reduce-scatter.14
  411.3 60.8 reduce-scatter.10
  474.4 41.8 all-gather.4
where the time goes:
time: 527 us; the launch traced here: 526 us
  waiting for transfers between devices  324 us (61%)
  blocking collectives  127 us (24%)
  matrix products  29.9 us (6%)
  other arithmetic  25.8 us (5%)
  between operations  14.2 us (3%)
  local copies, waits for them, and re-layouts  5.53 us (1%)
    reduce_scatter x2, waiting for transfers between devices, per_device(): lax.psum_scatter(sums, 'dp', scatter_dimension=0, tiled=True)  125 us
    unnamed x8, waiting for transfers between devices  113 us
    all_gather x2, waiting for transfers between devices, per_device(): current = lax.all_gather(fresh, 'dp', axis=0, tiled=True)  84.9 us
    pmax x2, blocking collectives, per_device(): highest = lax.pmax(local_top, 'cent')  68.4 us
    psum x2, blocking collectives, per_device(): lax.psum(jnp.sum(jnp.exp(scores - highest[:, None]), axis=1), 'cent')  58.5 us
    dot_general x2, matrix products, per_device(): lax.dot_general(weights, embeds, (((0,), (0,)), ((), ())), preferred_elem...  15.9 us
    dot_general x2, matrix products, per_device(): jnp.dot(embeds, current.T, preferred_element_type=jnp.float32)  14 us
  transfers between devices with their start and end apart: 6, of which 6 were waited for; matrix products, arithmetic and copies ran while one was open for 3% of the time, Pallas kernels for 0%

commit v1 on v0

v1 whole, which is shorter than its diff:
```python
import functools
import math

import jax
import jax.numpy as jnp
from jax import lax
from jax.experimental import pallas as pl
from jax.experimental.pallas import tpu as pltpu
from jax.sharding import PartitionSpec as P

ITERS = 2
TEMP = 2.5
D = 1024
ROWS = 1536
CENTS = 1024
NZ = 8
NC = 16
OWN = CENTS // 2
CHUNK = OWN // NZ
HALF = CHUNK // 2
GROUP = OWN // 2
RB = 512
KEXP = TEMP * math.log2(math.e)
LN2 = math.log(2.0)

OFF = (4, 3, 5, 2, 6, 1, 7, 0)
SLOT = {o: j for j, o in enumerate(OFF)}
CHAINS = ((1, 0, 4), (-1, 1, 4), (1, 1, 3), (-1, 0, 3))
MSG = {}
for _c, (_d, _h, _l) in enumerate(CHAINS):
    for _k in range(_l):
        MSG[(_c, _k)] = len(MSG)
NMSG = len(MSG)
MESH = pl.DeviceIdType.MESH
F32 = jnp.float32
BF16 = jnp.bfloat16


def nt_dot(a, b):
    return lax.dot_general(a, b, (((1,), (1,)), ((), ())), preferred_element_type=F32)


def lse2(parts):
    top = functools.reduce(jnp.maximum, parts)
    return top + jnp.log2(sum(jnp.exp2(p - top) for p in parts))


def kernel(
    emb, cen, out, row_lse,
    E, CUR, CO, PB, W, SUMS, MG, LOC, XS, XR, SS, SR, MACC, MS, MR, RSB, RRB,
    ld_e, ld_c, es_s, es_r, x_s, x_r, s_s, s_r, m_s, m_r, rs_s, rs_r, ag_s, ag_r, o_l, o_s, o_r,
):
    dp = lax.axis_index("dp")
    cent = lax.axis_index("cent")
    z = dp // 2
    core = dp % 2
    sib = (z * 2 + (1 - core), cent)

    def zdev(h):
        return (((z + h + NZ) % NZ) * 2 + core, cent)

    def cdev(k):
        return (dp, (cent + k) % NC)

    def remote(src, dst, s, r, dev):
        return pltpu.make_async_remote_copy(
            src_ref=src, dst_ref=dst, send_sem=s, recv_sem=r, device_id=dev, device_id_type=MESH
        )

    def chunk_row(j):
        return pl.multiple_of(core * OWN + ((z + OFF[j]) % NZ) * CHUNK, CHUNK)

    barrier = pltpu.get_barrier_semaphore()
    pl.semaphore_signal(barrier, inc=1, device_id=sib, device_id_type=MESH)
    for k in range(1, NC):
        pl.semaphore_signal(barrier, inc=1, device_id=cdev(k), device_id_type=MESH)
    for h in range(1, NZ):
        pl.semaphore_signal(barrier, inc=1, device_id=zdev(h), device_id_type=MESH)

    load_c = [
        pltpu.make_async_copy(cen.at[pl.ds(chunk_row(j), CHUNK)], CUR.at[0, pl.ds(j * CHUNK, CHUNK)], ld_c.at[j])
        for j in range(NZ)
    ]
    load_c.append(
        pltpu.make_async_copy(cen.at[pl.ds(pl.multiple_of((1 - core) * OWN, OWN), OWN)], CO, ld_c.at[NZ])
    )
    nb = ROWS // RB
    load_e = [
        pltpu.make_async_copy(emb.at[pl.ds(b * RB, RB)], E.at[pl.ds(b * RB, RB)], ld_e.at[b]) for b in range(nb)
    ]
    for c in load_c[:NZ]:
        c.start()
    load_e[0].start()
    load_c[NZ].start()
    for c in load_e[1:]:
        c.start()

    pl.semaphore_wait(barrier, NC - 1 + NZ - 1 + 1)
    send_e = [
        remote(emb.at[pl.ds(b * RB, RB)], E.at[pl.ds(ROWS + b * RB, RB)], es_s.at[b], es_r.at[b], sib)
        for b in range(nb)
    ]
    for c in send_e:
        c.start()
    for c in load_c:
        c.wait()
    for c in load_e:
        c.wait()

    def half_norm(c):
        return (0.5 * KEXP) * jnp.sum(jnp.square(c.astype(F32)), axis=1, keepdims=True)

    def block(c, n, r0):
        s = KEXP * nt_dot(c, E[pl.ds(r0, RB), :]) - n
        m = jnp.max(s, axis=0, keepdims=True)
        p = jnp.exp2(s - m)
        return p, m, m + jnp.log2(jnp.sum(p, axis=0, keepdims=True))

    def own_groups(turn, r0):
        lses = []
        for g in range(2):
            c = CUR[turn, pl.ds(g * GROUP, GROUP), :]
            p, m, l = block(c, half_norm(c), r0)
            PB[pl.ds(g * GROUP, GROUP), pl.ds(r0, RB)] = p
            MG[g, :, pl.ds(r0, RB)] = m
            lses.append(l)
        return lses

    for turn in range(ITERS):
        if turn == 0:

            @pl.loop(0, nb)
            def _(b):
                r0 = pl.multiple_of(b * RB, RB)
                lses = own_groups(0, r0)
                for g in range(2):
                    c = CO[pl.ds(g * GROUP, GROUP), :]
                    lses.append(block(c, half_norm(c), r0)[2])
                XS[turn, :, pl.ds(r0, RB)] = lse2(lses)

        else:

            @pl.loop(nb, 2 * nb)
            def _(b):
                r0 = pl.multiple_of(b * RB, RB)
                LOC[:, pl.ds(r0, RB)] = lse2(own_groups(turn, r0))

            part = remote(LOC.at[:, pl.ds(ROWS, ROWS)], SR.at[0], s_s.at[0], s_r.at[0], sib)
            part.start()

            @pl.loop(0, nb)
            def _(b):
                r0 = pl.multiple_of(b * RB, RB)
                LOC[:, pl.ds(r0, RB)] = lse2(own_groups(turn, r0))

            part.wait()
            XS[turn] = lse2([LOC[:, pl.ds(0, ROWS)], SR[0]])

        sends = [
            remote(XS.at[turn], XR.at[turn, k - 1], x_s.at[turn, k - 1], x_r.at[turn, k - 1], cdev(k))
            for k in range(1, NC)
        ]
        for c in sends:
            c.start()
        if turn == 0:
            for c in send_e:
                c.wait()

            @pl.loop(nb, 2 * nb)
            def _(b):
                own_groups(0, pl.multiple_of(b * RB, RB))

        for c in sends:
            c.wait()
        total = lse2([XS[turn]] + [XR[turn, k] for k in range(NC - 1)])
        SS[turn] = total
        LOC[:, pl.ds(0, ROWS)] = total
        back = remote(SS.at[turn], SR.at[1 + turn], s_s.at[1 + turn], s_r.at[1 + turn], sib)
        back.start()
        if turn == ITERS - 1:
            row_lse[...] = total * LN2

        MACC[...] = jnp.zeros_like(MACC)

        def weights(b):
            r0 = pl.multiple_of(b * RB, RB)
            lse = LOC[:, pl.ds(r0, RB)]
            for g in range(2):
                rows = pl.ds(g * GROUP, GROUP)
                w = (PB[rows, pl.ds(r0, RB)] * jnp.exp2(MG[g, :, pl.ds(r0, RB)] - lse)).astype(BF16)
                W[rows, pl.ds(r0, RB)] = w
                wf = w.astype(F32)
                MACC[rows, :] += sum(wf[:, i * 128 : (i + 1) * 128] for i in range(RB // 128))

        pl.loop(0, nb)(weights)
        back.wait()
        LOC[:, pl.ds(ROWS, ROWS)] = SR[1 + turn]
        pl.loop(nb, 2 * nb)(weights)
        MS[turn] = jnp.sum(MACC[...].T, axis=0, keepdims=True)
        masses = [
            remote(MS.at[turn], MR.at[turn, h - 1], m_s.at[turn, h - 1], m_r.at[turn, h - 1], zdev(h))
            for h in range(1, NZ)
        ]
        for c in masses:
            c.start()

        for g in range(2):

            @pl.loop(0, D // 256)
            def _(n):
                cols = pl.ds(pl.multiple_of(n * 256, 256), 256)
                SUMS[pl.ds(g * GROUP, GROUP), cols] = jnp.dot(
                    W[pl.ds(g * GROUP, GROUP), :], E[:, cols], preferred_element_type=F32
                )

        ring = {
            (c, k): remote(
                RSB.at[turn, MSG[c, k]], RRB.at[turn, MSG[c, k]],
                rs_s.at[turn, MSG[c, k]], rs_r.at[turn, MSG[c, k]], zdev(CHAINS[c][0]),
            )
            for c, k in MSG
        }
        for k in range(4):
            for c, (d, h, hops) in enumerate(CHAINS):
                if k < hops:
                    o = (d * (hops - k)) % NZ
                    v = SUMS[pl.ds(SLOT[o] * CHUNK + h * HALF, HALF), :]
                    if k:
                        ring[c, k - 1].wait_recv()
                        v = v + RRB[turn, MSG[c, k - 1]].astype(F32)
                    RSB[turn, MSG[c, k]] = v.astype(BF16)
                    ring[c, k].start()
        for c in masses:
            c.wait()
        lane = lax.broadcasted_iota(jnp.int32, (CHUNK, 128), 1)
        row = lax.broadcasted_iota(jnp.int32, (CHUNK, 128), 0)
        acc = jnp.zeros((CHUNK, 128), F32)
        for h in range(NZ):
            j = SLOT[h]
            vec = MS[turn] if h == 0 else MR[turn, h - 1]
            vec = vec[:, (j // 2) * 128 : (j // 2 + 1) * 128]
            acc = acc + jnp.where(lane == row + CHUNK * (j % 2), jnp.broadcast_to(vec, (CHUNK, 128)), 0.0)
        inv = 1.0 / (jnp.sum(acc, axis=1, keepdims=True) + 1.0)

        gather = {}
        for c, (d, h, hops) in enumerate(CHAINS):
            for k in range(hops):
                src = CUR.at[turn + 1, pl.ds(SLOT[(-d * k) % NZ] * CHUNK + h * HALF, HALF)]
                dst = CUR.at[turn + 1, pl.ds(SLOT[(-d * (k + 1)) % NZ] * CHUNK + h * HALF, HALF)]
                i = MSG[c, k]
                gather[c, k] = remote(src, dst, ag_s.at[turn, i], ag_r.at[turn, i], zdev(d))
        last_hop = {0: ((0, 3), (3, 2)), 1: ((1, 3), (2, 2))}
        for h in range(2):
            rows = pl.ds(SLOT[0] * CHUNK + h * HALF, HALF)
            v = SUMS[rows, :] + CUR[turn, rows, :].astype(F32)
            for c, k in last_hop[h]:
                ring[c, k].wait_recv()
                v = v + RRB[turn, MSG[c, k]].astype(F32)
            CUR[turn + 1, rows, :] = (v * inv[h * HALF : (h + 1) * HALF]).astype(BF16)
            for c in range(4):
                if CHAINS[c][1] == h:
                    gather[c, 0].start()
        for k in range(1, 4):
            for c, (d, h, hops) in enumerate(CHAINS):
                if k < hops:
                    gather[c, k - 1].wait_recv()
                    gather[c, k].start()
        for c, (d, h, hops) in enumerate(CHAINS):
            gather[c, hops - 1].wait_recv()
        for c, k in MSG:
            ring[c, k].wait_send()
            gather[c, k].wait_send()

    stores = []
    for j in range(NZ):
        src = CUR.at[ITERS, pl.ds(j * CHUNK, CHUNK)]
        dst = out.at[pl.ds(chunk_row(j), CHUNK)]
        stores.append(pltpu.make_async_copy(src, dst, o_l.at[j]))
        stores.append(remote(src, dst, o_s.at[j], o_r.at[j], sib))
    for c in stores:
        c.start()
    for c in stores:
        c.wait()


def per_device(embeds, centroids):
    dma = pltpu.SemaphoreType.DMA
    new, lse = pl.pallas_call(
        kernel,
        out_shape=(
            jax.ShapeDtypeStruct((CENTS, D), BF16),
            jax.ShapeDtypeStruct((1, ROWS), F32),
        ),
        in_specs=[pl.BlockSpec(memory_space=pl.ANY)] * 2,
        out_specs=(pl.BlockSpec(memory_space=pl.ANY), pl.BlockSpec(memory_space=pltpu.VMEM)),
        scratch_shapes=[
            pltpu.VMEM((2 * ROWS, D), BF16),
            pltpu.VMEM((ITERS + 1, OWN, D), BF16),
            pltpu.VMEM((OWN, D), BF16),
            pltpu.VMEM((OWN, 2 * ROWS), F32),
            pltpu.VMEM((OWN, 2 * ROWS), BF16),
            pltpu.VMEM((OWN, D), F32),
            pltpu.VMEM((2, 1, 2 * ROWS), F32),
            pltpu.VMEM((1, 2 * ROWS), F32),
            pltpu.VMEM((ITERS, 1, ROWS), F32),
            pltpu.VMEM((ITERS, NC - 1, 1, ROWS), F32),
            pltpu.VMEM((ITERS, 1, ROWS), F32),
            pltpu.VMEM((ITERS + 1, 1, ROWS), F32),
            pltpu.VMEM((OWN, 128), F32),
            pltpu.VMEM((ITERS, 1, OWN), F32),
            pltpu.VMEM((ITERS, NZ - 1, 1, OWN), F32),
            pltpu.VMEM((ITERS, NMSG, HALF, D), BF16),
            pltpu.VMEM((ITERS, NMSG, HALF, D), BF16),
            dma((ROWS // RB,)),
            dma((NZ + 1,)),
            dma((ROWS // RB,)),
            dma((ROWS // RB,)),
            dma((ITERS, NC - 1)),
            dma((ITERS, NC - 1)),
            dma((ITERS + 1,)),
            dma((ITERS + 1,)),
            dma((ITERS, NZ - 1)),
            dma((ITERS, NZ - 1)),
            dma((ITERS, NMSG)),
            dma((ITERS, NMSG)),
            dma((ITERS, NMSG)),
            dma((ITERS, NMSG)),
            dma((NZ,)),
            dma((NZ,)),
            dma((NZ,)),
        ],
        compiler_params=pltpu.CompilerParams(
            collective_id=0, has_side_effects=True, vmem_limit_bytes=56 * 1024 * 1024
        ),
    )(embeds, centroids)
    return new, lse.reshape(ROWS)


def solution(mesh):
    return jax.shard_map(
        per_device,
        mesh=mesh,
        in_specs=(P("dp", None), P("cent", None)),
        out_specs=(P("cent", None), P("dp")),
        check_vma=False,
    )
```

time: 527 us -> 118 us (0.22)
  waiting for transfers between devices: 324 us -> 0 us
  blocking collectives: 127 us -> 0 us
  Pallas kernels: 0 us -> 112 us
  matrix products: 29.9 us -> 0 us
  other arithmetic: 25.8 us -> 1.31 us
  between operations: 14.2 us -> 0.64 us
    reduce_scatter x2 -> x0, waiting for transfers between devices: 125 us -> none  [per_device(): lax.psum_scatter(sums, 'dp', scatter_dimension=0, tiled=True)]
    unnamed x8 -> x0, waiting for transfers between devices: 113 us -> none
    pallas_call x0 -> x1, Pallas kernels: none -> 112 us  [per_device(): pl.pallas_call(kernel, out_shape=(jax.ShapeDtypeStruct((CENTS, D), BF16),...]
    all_gather x2 -> x0, waiting for transfers between devices: 84.9 us -> none  [per_device(): current = lax.all_gather(fresh, 'dp', axis=0, tiled=True)]
    pmax x2 -> x0, blocking collectives: 68.4 us -> none  [per_device(): highest = lax.pmax(local_top, 'cent')]
    psum x2 -> x0, blocking collectives: 58.5 us -> none  [per_device(): lax.psum(jnp.sum(jnp.exp(scores - highest[:, None]), axis=1), 'cent')]
    dot_general x4 -> x0, matrix products: 29.9 us -> none  [the longest x2 15.9 us: per_device(): lax.dot_general(weights, embeds, (((0,), (0,)), ((), ())), preferred_elem...]
    reduce_sum x6 -> x0, other arithmetic: 20.8 us -> none  [the longest x2 8.31 us: per_device(): mass = jnp.sum(weights.astype(jnp.float32), axis=0)]
  transfers between devices with their start and end apart: 6 -> 0, of which waited for: 6 -> 0; matrix products, arithmetic and copies ran while one was open for 3% -> 0% of each run, Pallas kernels for 0% -> 0%
where the time goes in v1:
time: 118 us; the launch traced here: 117 us
  Pallas kernels  112 us (95%)
  local copies, waits for them, and re-layouts  3.08 us (3%)
  other arithmetic  1.31 us (1%)
    pallas_call x1, Pallas kernels, per_device(): pl.pallas_call(kernel, out_shape=(jax.ShapeDtypeStruct((CENTS, D), BF16),...  112 us
    unnamed x1, local copies, waits for them, and re-layouts  3.08 us

profile of v1, /device:TPU:1, one launch (start us, length us, event | category | flops | bytes accessed | tf_op | source)
XLA Modules:
  0.0 117.4 jit_solution(13990706428758207995)
XLA Ops:
  0.6 112.3 %shard_map.41 = (bf16[1024,1024]{1,0:T(8,128)(2,1)}, f32[1,1536]{1,0:T(1,128)}) custom-call(bf16[1536,1024]{1,0:T(8,128)(2,1)} %emb.1, bf16[1024,1024]{1,0:T(8,128)(2,1)} %cen.1), custom_call_target="tpu_custom_call" | custom-call | tf_op jit(solution)/shard_map/pallas_call | solution.py:288
  113.0 1.3 %reduce = f32[1536]{0:T(1024)} reduce(f32[1,1536]{1,0:T(1,128)} %get-tuple-element.5, f32[]{:T(128)} %constant), dimensions={0}, to_apply=%get-tuple-element.5.reduce_sub_computation | reduce | bytes 12292 | tf_op jit(solution)/shard_map/pallas_call | solution.py:288
  114.3 3.1 %copy.5 = bf16[1024,1024]{1,0:T(8,128)(2,1)} copy(bf16[1024,1024]{1,0:T(8,128)(2,1)} %get-tuple-element.8) | data formatting | bytes 4194304

commit v2 on v1

v2 whole, which is shorter than its diff:
```python
import functools
import math

import jax
import jax.numpy as jnp
from jax import lax
from jax.experimental import pallas as pl
from jax.experimental.pallas import tpu as pltpu
from jax.sharding import PartitionSpec as P

ITERS = 2
TEMP = 2.5
D = 1024
ROWS = 1536
CENTS = 1024
NZ = 8
NC = 16
OWN = CENTS // 2
CHUNK = OWN // NZ
WAVES = 2
PIECE = CHUNK // WAVES // 2
GROUP = OWN // 2
RB = 512
NB = ROWS // RB
KEXP = TEMP * math.log2(math.e)
LN2 = math.log(2.0)

OFF = (4, 3, 5, 2, 6, 1, 7, 0)
SLOT = {o: j for j, o in enumerate(OFF)}
CHAINS = ((1, 0, 4), (-1, 1, 4), (1, 1, 3), (-1, 0, 3))
MSG = {}
for _w in range(WAVES):
    for _c, (_d, _h, _l) in enumerate(CHAINS):
        for _k in range(_l):
            MSG[(_w, _c, _k)] = len(MSG)
NMSG = len(MSG)
MESH = pl.DeviceIdType.MESH
F32 = jnp.float32
BF16 = jnp.bfloat16


def nt_dot(a, b):
    return lax.dot_general(a, b, (((1,), (1,)), ((), ())), preferred_element_type=F32)


def lse2(parts):
    top = functools.reduce(jnp.maximum, parts)
    return top + jnp.log2(sum(jnp.exp2(p - top) for p in parts))


def kernel(
    emb, cen, out, row_lse,
    E, CUR, CO, NRM, NRO, PB, W, SUMS, MG, LG, LOC, XS, XR, SS, SR, MACC, MS, MR, RSB, RRB,
    ld_e, ld_c, es_s, es_r, x_s, x_r, s_s, s_r, m_s, m_r, rs_s, rs_r, ag_s, ag_r, o_l, o_s, o_r,
):
    dp = lax.axis_index("dp")
    cent = lax.axis_index("cent")
    z = dp // 2
    core = dp % 2
    sib = (z * 2 + (1 - core), cent)

    def zdev(h):
        return (((z + h + NZ) % NZ) * 2 + core, cent)

    def cdev(k):
        return (dp, (cent + k) % NC)

    def remote(src, dst, s, r, dev):
        return pltpu.make_async_remote_copy(
            src_ref=src, dst_ref=dst, send_sem=s, recv_sem=r, device_id=dev, device_id_type=MESH
        )

    def chunk_row(j):
        return pl.multiple_of(core * OWN + ((z + OFF[j]) % NZ) * CHUNK, CHUNK)

    barrier = pltpu.get_barrier_semaphore()
    pl.semaphore_signal(barrier, inc=1, device_id=sib, device_id_type=MESH)
    for k in range(1, NC):
        pl.semaphore_signal(barrier, inc=1, device_id=cdev(k), device_id_type=MESH)
    for h in range(1, NZ):
        pl.semaphore_signal(barrier, inc=1, device_id=zdev(h), device_id_type=MESH)

    load_c = [
        pltpu.make_async_copy(cen.at[pl.ds(chunk_row(j), CHUNK)], CUR.at[0, pl.ds(j * CHUNK, CHUNK)], ld_c.at[j])
        for j in range(NZ)
    ]
    load_c.append(
        pltpu.make_async_copy(cen.at[pl.ds(pl.multiple_of((1 - core) * OWN, OWN), OWN)], CO, ld_c.at[NZ])
    )
    load_e = [
        pltpu.make_async_copy(emb.at[pl.ds(b * RB, RB)], E.at[pl.ds(b * RB, RB)], ld_e.at[b]) for b in range(NB)
    ]
    for c in load_c[:NZ]:
        c.start()
    load_e[0].start()
    load_c[NZ].start()
    for c in load_e[1:]:
        c.start()

    pl.semaphore_wait(barrier, NC - 1 + NZ - 1 + 1)
    send_e = [
        remote(emb.at[pl.ds(b * RB, RB)], E.at[pl.ds(ROWS + b * RB, RB)], es_s.at[b], es_r.at[b], sib)
        for b in range(NB)
    ]
    for c in send_e:
        c.start()
    for c in load_c:
        c.wait()
    for c in load_e:
        c.wait()

    def store_norms(turn, g):
        c = CUR[turn, pl.ds(g * GROUP, GROUP), :]
        n = (0.5 * KEXP) * jnp.sum(jnp.square(c.astype(F32)), axis=1, keepdims=True)
        NRM[pl.ds(g * GROUP, GROUP), :] = jnp.broadcast_to(n, (GROUP, 128))

    def block(c, n, r0):
        s = KEXP * nt_dot(c, E[pl.ds(r0, RB), :]) - n
        m = jnp.max(s, axis=0, keepdims=True)
        p = jnp.exp2(s - m)
        return p, m, m + jnp.log2(jnp.sum(p, axis=0, keepdims=True))

    def wide(n):
        return jnp.concatenate([n] * (RB // 128), axis=1)

    def own_block(turn, g, b):
        r0 = pl.multiple_of(b * RB, RB)
        rows, cols = pl.ds(g * GROUP, GROUP), pl.ds(r0, RB)
        n = wide(NRM[rows, :])
        p, m, l = block(CUR[turn, rows, :], n, r0)
        PB[rows, cols] = p
        MG[g, :, cols] = m
        LG[g, :, cols] = l

    for g in range(2):
        store_norms(0, g)
        c = CO[pl.ds(g * GROUP, GROUP), :]
        n = (0.5 * KEXP) * jnp.sum(jnp.square(c.astype(F32)), axis=1, keepdims=True)
        NRO[pl.ds(g * GROUP, GROUP), :] = jnp.broadcast_to(n, (GROUP, 128))
    mine, theirs = pl.ds(0, ROWS), pl.ds(ROWS, ROWS)

    for turn in range(ITERS):
        last = turn == ITERS - 1
        if turn == 0:

            @pl.loop(0, NB)
            def _(b):
                r0 = pl.multiple_of(b * RB, RB)
                for g in range(2):
                    own_block(0, g, b)
                lses = [LG[g, :, pl.ds(r0, RB)] for g in range(2)]
                for g in range(2):
                    rows = pl.ds(g * GROUP, GROUP)
                    lses.append(block(CO[rows, :], wide(NRO[rows, :]), r0)[2])
                XS[turn, :, pl.ds(r0, RB)] = lse2(lses)

        else:
            pl.loop(NB, 2 * NB)(functools.partial(own_block, turn, 0))
            LOC[:, theirs] = lse2([LG[0, :, theirs], LG[1, :, theirs]])
            part = remote(LOC.at[:, theirs], SR.at[0], s_s.at[0], s_r.at[0], sib)
            part.start()
            pl.loop(0, NB)(functools.partial(own_block, turn, 0))
            both = lse2([LG[0, :, mine], LG[1, :, mine]])
            part.wait()
            XS[turn] = lse2([both, SR[0]])

        sends = [
            remote(XS.at[turn], XR.at[turn, k - 1], x_s.at[turn, k - 1], x_r.at[turn, k - 1], cdev(k))
            for k in range(1, NC)
        ]
        for c in sends:
            c.start()
        if turn == 0:
            for c in send_e:
                c.wait()

            @pl.loop(NB, 2 * NB)
            def _(b):
                for g in range(2):
                    own_block(0, g, b)

        for c in sends:
            c.wait()
        total = lse2([XS[turn]] + [XR[turn, k] for k in range(NC - 1)])
        SS[turn] = total
        LOC[:, mine] = total
        back = remote(SS.at[turn], SR.at[1 + turn], s_s.at[1 + turn], s_r.at[1 + turn], sib)
        back.start()
        MACC[...] = jnp.zeros_like(MACC)

        def weights(b):
            r0 = pl.multiple_of(b * RB, RB)
            lse = LOC[:, pl.ds(r0, RB)]
            for g in range(2):
                rows = pl.ds(g * GROUP, GROUP)
                w = (PB[rows, pl.ds(r0, RB)] * jnp.exp2(MG[g, :, pl.ds(r0, RB)] - lse)).astype(BF16)
                W[rows, pl.ds(r0, RB)] = w
                wf = w.astype(F32)
                MACC[rows, :] += sum(wf[:, i * 128 : (i + 1) * 128] for i in range(RB // 128))

        pl.loop(0, NB)(weights)
        back.wait()
        LOC[:, theirs] = SR[1 + turn]
        pl.loop(NB, 2 * NB)(weights)

        def sums(g):
            @pl.loop(0, D // 256)
            def _(n):
                cols = pl.ds(pl.multiple_of(n * 256, 256), 256)
                SUMS[pl.ds(g * GROUP, GROUP), cols] = jnp.dot(
                    W[pl.ds(g * GROUP, GROUP), :], E[:, cols], preferred_element_type=F32
                )

        ring = {
            (w, c, k): remote(
                RSB.at[turn, i], RRB.at[turn, i], rs_s.at[turn, i], rs_r.at[turn, i], zdev(CHAINS[c][0])
            )
            for (w, c, k), i in MSG.items()
        }

        def ring_hop(w, k):
            for c, (d, h, hops) in enumerate(CHAINS):
                if k < hops:
                    o = (d * (hops - k)) % NZ
                    v = SUMS[pl.ds(SLOT[o] * CHUNK + (2 * w + h) * PIECE, PIECE), :]
                    if k:
                        ring[w, c, k - 1].wait_recv()
                        v = v + RRB[turn, MSG[w, c, k - 1]].astype(F32)
                    RSB[turn, MSG[w, c, k]] = v.astype(BF16)
                    ring[w, c, k].start()

        sums(0)
        for w in range(WAVES):
            ring_hop(w, 0)
        sums(1)
        MS[turn] = jnp.sum(MACC[...].T, axis=0, keepdims=True)
        masses = [
            remote(MS.at[turn], MR.at[turn, h - 1], m_s.at[turn, h - 1], m_r.at[turn, h - 1], zdev(h))
            for h in range(1, NZ)
        ]
        for c in masses:
            c.start()
        for k in range(1, 4):
            for w in range(WAVES):
                ring_hop(w, k)
        for c in masses:
            c.wait()
        lane = lax.broadcasted_iota(jnp.int32, (CHUNK, 128), 1)
        row = lax.broadcasted_iota(jnp.int32, (CHUNK, 128), 0)
        acc = jnp.zeros((CHUNK, 128), F32)
        for h in range(NZ):
            j = SLOT[h]
            vec = MS[turn] if h == 0 else MR[turn, h - 1]
            vec = vec[:, (j // 2) * 128 : (j // 2 + 1) * 128]
            acc = acc + jnp.where(lane == row + CHUNK * (j % 2), jnp.broadcast_to(vec, (CHUNK, 128)), 0.0)
        inv = 1.0 / (jnp.sum(acc, axis=1, keepdims=True) + 1.0)

        def place(o, piece):
            start = piece * PIECE
            if last:
                return out.at[pl.ds(pl.multiple_of(chunk_row(SLOT[o % NZ]) + start, PIECE), PIECE)]
            return CUR.at[turn + 1, pl.ds(SLOT[o % NZ] * CHUNK + start, PIECE)]

        gather, pairs, keeps = {}, {}, []
        for (w, c, k), i in MSG.items():
            d, h, hops = CHAINS[c]
            piece = 2 * w + h
            src = place(-d * k, piece)
            dst = src if last else place(-d * (k + 1), piece)
            if last and k == 0:
                src = CUR.at[0, pl.ds(piece * PIECE, PIECE)]
            gather[w, c, k] = remote(src, dst, ag_s.at[turn, i], ag_r.at[turn, i], zdev(d))
            if last:
                got = place(-d * (k + 1), 2 * w + h)
                pairs[w, c, k] = remote(got, got, o_s.at[i], o_r.at[i], sib)
        if last:
            for w in range(WAVES):
                start = 2 * w * PIECE
                fresh = CUR.at[0, pl.ds(start, 2 * PIECE)]
                rows = out.at[pl.ds(pl.multiple_of(chunk_row(SLOT[0]) + start, 2 * PIECE), 2 * PIECE)]
                pairs[w] = remote(fresh, rows, o_s.at[NMSG + w], o_r.at[NMSG + w], sib)
                keeps.append(pltpu.make_async_copy(fresh, rows, o_l.at[w]))

        def finish(w):
            for h in range(2):
                piece = 2 * w + h
                rows = pl.ds(SLOT[0] * CHUNK + piece * PIECE, PIECE)
                v = SUMS[rows, :] + CUR[turn, rows, :].astype(F32)
                for c in range(4):
                    if CHAINS[c][1] == h:
                        k = CHAINS[c][2] - 1
                        ring[w, c, k].wait_recv()
                        v = v + RRB[turn, MSG[w, c, k]].astype(F32)
                fresh = (v * inv[piece * PIECE : (piece + 1) * PIECE]).astype(BF16)
                if last:
                    CUR[0, pl.ds(piece * PIECE, PIECE), :] = fresh
                else:
                    CUR[turn + 1, rows, :] = fresh
                for c in range(4):
                    if CHAINS[c][1] == h:
                        gather[w, c, 0].start()
            if last:
                pairs[w].start()
                keeps[w].start()

        def gather_hop(w, k):
            for c, (d, h, hops) in enumerate(CHAINS):
                if k <= hops:
                    gather[w, c, k - 1].wait_recv()
                    if k < hops:
                        gather[w, c, k].start()
                    if last:
                        pairs[w, c, k - 1].start()

        for w in range(WAVES):
            finish(w)
        for k in (1, 2):
            for w in range(WAVES):
                gather_hop(w, k)
        if last:
            for k in (3, 4):
                for w in range(WAVES):
                    gather_hop(w, k)
            row_lse[...] = (SS[turn] * LN2).reshape(ROWS)
        else:
            store_norms(turn + 1, 1)
            near = functools.partial(own_block, turn + 1, 1)
            pl.loop(0, 2)(near)
            gather_hop(0, 3)
            gather_hop(1, 3)
            pl.loop(2, 4)(near)
            gather_hop(0, 4)
            gather_hop(1, 4)
            pl.loop(4, 6)(near)
            store_norms(turn + 1, 0)
        for key in MSG:
            ring[key].wait_send()
            gather[key].wait_send()

    for c in list(pairs.values()) + keeps:
        c.wait()


def per_device(embeds, centroids):
    dma = pltpu.SemaphoreType.DMA
    new, lse = pl.pallas_call(
        kernel,
        out_shape=(
            jax.ShapeDtypeStruct((CENTS, D), BF16),
            jax.ShapeDtypeStruct((ROWS,), F32),
        ),
        in_specs=[pl.BlockSpec(memory_space=pltpu.HBM)] * 2,
        out_specs=(pl.BlockSpec(memory_space=pl.ANY), pl.BlockSpec(memory_space=pltpu.VMEM)),
        scratch_shapes=[
            pltpu.VMEM((2 * ROWS, D), BF16),
            pltpu.VMEM((ITERS, OWN, D), BF16),
            pltpu.VMEM((OWN, D), BF16),
            pltpu.VMEM((OWN, 128), F32),
            pltpu.VMEM((OWN, 128), F32),
            pltpu.VMEM((OWN, 2 * ROWS), F32),
            pltpu.VMEM((OWN, 2 * ROWS), BF16),
            pltpu.VMEM((OWN, D), F32),
            pltpu.VMEM((2, 1, 2 * ROWS), F32),
            pltpu.VMEM((2, 1, 2 * ROWS), F32),
            pltpu.VMEM((1, 2 * ROWS), F32),
            pltpu.VMEM((ITERS, 1, ROWS), F32),
            pltpu.VMEM((ITERS, NC - 1, 1, ROWS), F32),
            pltpu.VMEM((ITERS, 1, ROWS), F32),
            pltpu.VMEM((ITERS + 1, 1, ROWS), F32),
            pltpu.VMEM((OWN, 128), F32),
            pltpu.VMEM((ITERS, 1, OWN), F32),
            pltpu.VMEM((ITERS, NZ - 1, 1, OWN), F32),
            pltpu.VMEM((ITERS, NMSG, PIECE, D), BF16),
            pltpu.VMEM((ITERS, NMSG, PIECE, D), BF16),
            dma((ROWS // RB,)),
            dma((NZ + 1,)),
            dma((ROWS // RB,)),
            dma((ROWS // RB,)),
            dma((ITERS, NC - 1)),
            dma((ITERS, NC - 1)),
            dma((ITERS + 1,)),
            dma((ITERS + 1,)),
            dma((ITERS, NZ - 1)),
            dma((ITERS, NZ - 1)),
            dma((ITERS, NMSG)),
            dma((ITERS, NMSG)),
            dma((ITERS, NMSG)),
            dma((ITERS, NMSG)),
            dma((WAVES,)),
            dma((NMSG + WAVES,)),
            dma((NMSG + WAVES,)),
        ],
        compiler_params=pltpu.CompilerParams(
            collective_id=0, has_side_effects=True, vmem_limit_bytes=50 * 1024 * 1024
        ),
    )(embeds, centroids)
    return new, lse


def solution(mesh):
    return jax.shard_map(
        per_device,
        mesh=mesh,
        in_specs=(P("dp", None), P("cent", None)),
        out_specs=(P("cent", None), P("dp")),
        check_vma=False,
    )
```

time: 118 us -> 103 us (0.87)
  Pallas kernels: 112 us -> 100 us
  other arithmetic: 1.31 us -> 0 us
    pallas_call x1, Pallas kernels: 112 us -> 100 us  [per_device(): pl.pallas_call(kernel, out_shape=(jax.ShapeDtypeStruct((CENTS, D), BF16),...]
    pallas_call x1 -> x0, other arithmetic: 1.31 us -> none  [per_device(): pl.pallas_call(kernel, out_shape=(jax.ShapeDtypeStruct((CENTS, D), BF16),...]
    unnamed x1 -> x2, local copies, waits for them, and re-layouts: 3.08 us -> 1.92 us
where the time goes in v2:
time: 103 us
  Pallas kernels  100 us (97%)
  local copies, waits for them, and re-layouts  1.92 us (2%)
    pallas_call x1, Pallas kernels, per_device(): pl.pallas_call(kernel, out_shape=(jax.ShapeDtypeStruct((CENTS, D), BF16),...  100 us

profile of v2, /device:TPU:1, one launch (start us, length us, event | category | flops | bytes accessed | tf_op | source)
XLA Modules:
  0.0 102.8 jit_solution(3013475422376953100)
XLA Ops:
  0.6 100.2 %shard_map.41 = (bf16[1024,1024]{1,0:T(8,128)(2,1)S(1)}, f32[1536]{0:T(1024)S(1)}) custom-call(bf16[1536,1024]{1,0:T(8,128)(2,1)} %emb.1, bf16[1024,1024]{1,0:T(8,128)(2,1)} %cen.1), custom_call_target="tpu_custom_call" | custom-call | tf_op jit(solution)/shard_map/pallas_call | solution.py:346
  100.9 1.3 %copy.6 = bf16[1024,1024]{1,0:T(8,128)(2,1)} copy(bf16[1024,1024]{1,0:T(8,128)(2,1)S(1)} %get-tuple-element.4) | data formatting | bytes 4194304
  102.2 0.6 copy.7

commit v3 on v2

--- a/solution.py
+++ b/solution.py
@@ -20,7 +20,7 @@
 WAVES = 2
 PIECE = CHUNK // WAVES // 2
 GROUP = OWN // 2
-RB = 512
+RB = 768
 NB = ROWS // RB
 KEXP = TEMP * math.log2(math.e)
 LN2 = math.log(2.0)
@@ -50,7 +50,7 @@
 
 def kernel(
     emb, cen, out, row_lse,
-    E, CUR, CO, NRM, NRO, PB, W, SUMS, MG, LG, LOC, XS, XR, SS, SR, MACC, MS, MR, RSB, RRB,
+    E, CUR, CO, NRM, NRO, PB, W, SUMS, SB, MG, LG, LOC, XS, XR, SS, SR, MACC, MS, MR, RSB, RRB,
     ld_e, ld_c, es_s, es_r, x_s, x_r, s_s, s_r, m_s, m_r, rs_s, rs_r, ag_s, ag_r, o_l, o_s, o_r,
 ):
     dp = lax.axis_index("dp")
@@ -96,70 +96,68 @@
     load_c[NZ].start()
     for c in load_e[1:]:
         c.start()
-
-    pl.semaphore_wait(barrier, NC - 1 + NZ - 1 + 1)
     send_e = [
         remote(emb.at[pl.ds(b * RB, RB)], E.at[pl.ds(ROWS + b * RB, RB)], es_s.at[b], es_r.at[b], sib)
         for b in range(NB)
     ]
-    for c in send_e:
-        c.start()
+
+    def meet():
+        pl.semaphore_wait(barrier, NC - 1 + NZ - 1 + 1)
+        for c in send_e:
+            c.start()
+
+    def store_norms(dst, src, g):
+        rows = pl.ds(g * GROUP, GROUP)
+        n = (0.5 * KEXP) * jnp.sum(jnp.square(src[rows, :].astype(F32)), axis=1, keepdims=True)
+        dst[rows, :] = jnp.broadcast_to(n, (GROUP, 128))
+
+    def run_scores(items, hooks):
+        def product(i):
+            if i in hooks:
+                hooks[i]()
+            c, _, g, r0, _, _ = items[i]
+            SB[i % 2] = nt_dot(c[pl.ds(g * GROUP, GROUP), :], E[pl.ds(r0, RB), :])
+
+        product(0)
+        for i, (_, norms, g, r0, slot, keep) in enumerate(items):
+            if i + 1 < len(items):
+                product(i + 1)
+            rows, cols = pl.ds(g * GROUP, GROUP), pl.ds(r0, RB)
+            s = KEXP * SB[i % 2] - jnp.concatenate([norms[rows, :]] * (RB // 128), axis=1)
+            m = jnp.max(s, axis=0, keepdims=True)
+            p = jnp.exp2(s - m)
+            LG[slot, :, cols] = m + jnp.log2(jnp.sum(p, axis=0, keepdims=True))
+            if keep:
+                PB[rows, cols] = p
+                MG[g, :, cols] = m
+
+    def own_items(turn, groups, starts):
+        return [(CUR.at[turn], NRM, g, r0, g, True) for r0 in starts for g in groups]
+
+    mine_at, theirs_at = range(0, ROWS, RB), range(ROWS, 2 * ROWS, RB)
     for c in load_c:
         c.wait()
-    for c in load_e:
-        c.wait()
-
-    def store_norms(turn, g):
-        c = CUR[turn, pl.ds(g * GROUP, GROUP), :]
-        n = (0.5 * KEXP) * jnp.sum(jnp.square(c.astype(F32)), axis=1, keepdims=True)
-        NRM[pl.ds(g * GROUP, GROUP), :] = jnp.broadcast_to(n, (GROUP, 128))
-
-    def block(c, n, r0):
-        s = KEXP * nt_dot(c, E[pl.ds(r0, RB), :]) - n
-        m = jnp.max(s, axis=0, keepdims=True)
-        p = jnp.exp2(s - m)
-        return p, m, m + jnp.log2(jnp.sum(p, axis=0, keepdims=True))
-
-    def wide(n):
-        return jnp.concatenate([n] * (RB // 128), axis=1)
-
-    def own_block(turn, g, b):
-        r0 = pl.multiple_of(b * RB, RB)
-        rows, cols = pl.ds(g * GROUP, GROUP), pl.ds(r0, RB)
-        n = wide(NRM[rows, :])
-        p, m, l = block(CUR[turn, rows, :], n, r0)
-        PB[rows, cols] = p
-        MG[g, :, cols] = m
-        LG[g, :, cols] = l
-
     for g in range(2):
-        store_norms(0, g)
-        c = CO[pl.ds(g * GROUP, GROUP), :]
-        n = (0.5 * KEXP) * jnp.sum(jnp.square(c.astype(F32)), axis=1, keepdims=True)
-        NRO[pl.ds(g * GROUP, GROUP), :] = jnp.broadcast_to(n, (GROUP, 128))
+        store_norms(NRM, CUR.at[0], g)
+        store_norms(NRO, CO, g)
+    load_e[0].wait()
     mine, theirs = pl.ds(0, ROWS), pl.ds(ROWS, ROWS)
 
     for turn in range(ITERS):
         last = turn == ITERS - 1
         if turn == 0:
-
-            @pl.loop(0, NB)
-            def _(b):
-                r0 = pl.multiple_of(b * RB, RB)
-                for g in range(2):
-                    own_block(0, g, b)
-                lses = [LG[g, :, pl.ds(r0, RB)] for g in range(2)]
-                for g in range(2):
-                    rows = pl.ds(g * GROUP, GROUP)
-                    lses.append(block(CO[rows, :], wide(NRO[rows, :]), r0)[2])
-                XS[turn, :, pl.ds(r0, RB)] = lse2(lses)
-
+            items = []
+            for r0 in mine_at:
+                items += own_items(0, range(2), [r0])
+                items += [(CO, NRO, g, r0, 2 + g, False) for g in range(2)]
+            run_scores(items, {2: meet, 4: load_e[1].wait})
+            XS[turn] = lse2([LG[i, :, mine] for i in range(4)])
         else:
-            pl.loop(NB, 2 * NB)(functools.partial(own_block, turn, 0))
+            run_scores(own_items(turn, [0], theirs_at), {})
             LOC[:, theirs] = lse2([LG[0, :, theirs], LG[1, :, theirs]])
             part = remote(LOC.at[:, theirs], SR.at[0], s_s.at[0], s_r.at[0], sib)
             part.start()
-            pl.loop(0, NB)(functools.partial(own_block, turn, 0))
+            run_scores(own_items(turn, [0], mine_at), {})
             both = lse2([LG[0, :, mine], LG[1, :, mine]])
             part.wait()
             XS[turn] = lse2([both, SR[0]])
@@ -171,13 +169,8 @@
         for c in sends:
             c.start()
         if turn == 0:
-            for c in send_e:
-                c.wait()
-
-            @pl.loop(NB, 2 * NB)
-            def _(b):
-                for g in range(2):
-                    own_block(0, g, b)
+            send_e[0].wait()
+            run_scores(own_items(0, range(2), theirs_at), {2: send_e[1].wait})
 
         for c in sends:
             c.wait()
@@ -188,8 +181,7 @@
         back.start()
         MACC[...] = jnp.zeros_like(MACC)
 
-        def weights(b):
-            r0 = pl.multiple_of(b * RB, RB)
+        def weights(r0):
             lse = LOC[:, pl.ds(r0, RB)]
             for g in range(2):
                 rows = pl.ds(g * GROUP, GROUP)
@@ -198,19 +190,19 @@
                 wf = w.astype(F32)
                 MACC[rows, :] += sum(wf[:, i * 128 : (i + 1) * 128] for i in range(RB // 128))
 
-        pl.loop(0, NB)(weights)
+        def sums(q, depth, add=False):
+            rows = pl.ds(q * 2 * CHUNK, 2 * CHUNK)
+            v = jnp.dot(W[rows, depth], E[depth, :], preferred_element_type=F32)
+            SUMS[rows, :] = SUMS[rows, :] + v if add else v
+
+        for r0 in mine_at:
+            weights(r0)
+        for q in range(2):
+            sums(q, mine)
         back.wait()
         LOC[:, theirs] = SR[1 + turn]
-        pl.loop(NB, 2 * NB)(weights)
-
-        def sums(g):
-            @pl.loop(0, D // 256)
-            def _(n):
-                cols = pl.ds(pl.multiple_of(n * 256, 256), 256)
-                SUMS[pl.ds(g * GROUP, GROUP), cols] = jnp.dot(
-                    W[pl.ds(g * GROUP, GROUP), :], E[:, cols], preferred_element_type=F32
-                )
-
+        for r0 in theirs_at:
+            weights(r0)
         ring = {
             (w, c, k): remote(
                 RSB.at[turn, i], RRB.at[turn, i], rs_s.at[turn, i], rs_r.at[turn, i], zdev(CHAINS[c][0])
@@ -218,9 +210,9 @@
             for (w, c, k), i in MSG.items()
         }
 
-        def ring_hop(w, k):
+        def ring_hop(w, k, chains=range(4)):
             for c, (d, h, hops) in enumerate(CHAINS):
-                if k < hops:
+                if k < hops and c in chains:
                     o = (d * (hops - k)) % NZ
                     v = SUMS[pl.ds(SLOT[o] * CHUNK + (2 * w + h) * PIECE, PIECE), :]
                     if k:
@@ -229,10 +221,14 @@
                     RSB[turn, MSG[w, c, k]] = v.astype(BF16)
                     ring[w, c, k].start()
 
-        sums(0)
+        sums(0, theirs, add=True)
         for w in range(WAVES):
-            ring_hop(w, 0)
-        sums(1)
+            ring_hop(w, 0, (0, 1, 2))
+        sums(1, theirs, add=True)
+        for w in range(WAVES):
+            ring_hop(w, 0, (3,))
+        for q in (2, 3):
+            sums(q, pl.ds(0, 2 * ROWS))
         MS[turn] = jnp.sum(MACC[...].T, axis=0, keepdims=True)
         masses = [
             remote(MS.at[turn], MR.at[turn, h - 1], m_s.at[turn, h - 1], m_r.at[turn, h - 1], zdev(h))
@@ -323,16 +319,14 @@
                     gather_hop(w, k)
             row_lse[...] = (SS[turn] * LN2).reshape(ROWS)
         else:
-            store_norms(turn + 1, 1)
-            near = functools.partial(own_block, turn + 1, 1)
-            pl.loop(0, 2)(near)
+            store_norms(NRM, CUR.at[turn + 1], 1)
+            run_scores(own_items(turn + 1, [1], mine_at), {})
             gather_hop(0, 3)
             gather_hop(1, 3)
-            pl.loop(2, 4)(near)
+            run_scores(own_items(turn + 1, [1], theirs_at), {})
             gather_hop(0, 4)
             gather_hop(1, 4)
-            pl.loop(4, 6)(near)
-            store_norms(turn + 1, 0)
+            store_norms(NRM, CUR.at[turn + 1], 0)
         for key in MSG:
             ring[key].wait_send()
             gather[key].wait_send()
@@ -360,8 +354,9 @@
             pltpu.VMEM((OWN, 2 * ROWS), F32),
             pltpu.VMEM((OWN, 2 * ROWS), BF16),
             pltpu.VMEM((OWN, D), F32),
+            pltpu.VMEM((2, GROUP, RB), F32),
             pltpu.VMEM((2, 1, 2 * ROWS), F32),
-            pltpu.VMEM((2, 1, 2 * ROWS), F32),
+            pltpu.VMEM((4, 1, 2 * ROWS), F32),
             pltpu.VMEM((1, 2 * ROWS), F32),
             pltpu.VMEM((ITERS, 1, ROWS), F32),
             pltpu.VMEM((ITERS, NC - 1, 1, ROWS), F32),

time: 103 us -> 94.8 us (0.920)
  Pallas kernels: 100 us -> 92.2 us
    pallas_call x1, Pallas kernels: 100 us -> 92.2 us  [per_device(): pl.pallas_call(kernel, out_shape=(jax.ShapeDtypeStruct((CENTS, D), BF16),...]
where the time goes in v3:
time: 94.8 us
  Pallas kernels  92.2 us (97%)
  local copies, waits for them, and re-layouts  1.92 us (2%)
    pallas_call x1, Pallas kernels, per_device(): pl.pallas_call(kernel, out_shape=(jax.ShapeDtypeStruct((CENTS, D), BF16),...  92.2 us
    unnamed x2, local copies, waits for them, and re-layouts  1.92 us

profile of v3, /device:TPU:1, one launch (start us, length us, event | category | flops | bytes accessed | tf_op | source)
XLA Modules:
  0.0 94.8 jit_solution(5088468672461552306)
XLA Ops:
  0.6 92.2 %shard_map.41 = (bf16[1024,1024]{1,0:T(8,128)(2,1)S(1)}, f32[1536]{0:T(1024)S(1)}) custom-call(bf16[1536,1024]{1,0:T(8,128)(2,1)} %emb.1, bf16[1024,1024]{1,0:T(8,128)(2,1)} %cen.1), custom_call_target="tpu_custom_call" | custom-call | tf_op jit(solution)/shard_map/pallas_call | solution.py:340
  92.8 1.3 %copy.6 = bf16[1024,1024]{1,0:T(8,128)(2,1)} copy(bf16[1024,1024]{1,0:T(8,128)(2,1)S(1)} %get-tuple-element.4) | data formatting | bytes 4194304
  94.2 0.6 copy.7

commit v4 on v3

--- a/solution.py
+++ b/solution.py
@@ -34,6 +34,10 @@
         for _k in range(_l):
             MSG[(_w, _c, _k)] = len(MSG)
 NMSG = len(MSG)
+NX = NY = 4
+PEERS = [(dx, dy) for dx in range(NX) for dy in range(NY) if dx or dy]
+PEERS.sort(key=lambda p: -min(p[0], NX - p[0]) - min(p[1], NY - p[1]))
+ALONG = sorted(range(1, NZ), key=lambda h: -min(h, NZ - h))
 MESH = pl.DeviceIdType.MESH
 F32 = jnp.float32
 BF16 = jnp.bfloat16
@@ -63,7 +67,8 @@
         return (((z + h + NZ) % NZ) * 2 + core, cent)
 
     def cdev(k):
-        return (dp, (cent + k) % NC)
+        dx, dy = PEERS[k]
+        return (dp, ((cent // NY + dx) % NX) * NY + (cent % NY + dy) % NY)
 
     def remote(src, dst, s, r, dev):
         return pltpu.make_async_remote_copy(
@@ -75,9 +80,9 @@
 
     barrier = pltpu.get_barrier_semaphore()
     pl.semaphore_signal(barrier, inc=1, device_id=sib, device_id_type=MESH)
-    for k in range(1, NC):
+    for k in range(NC - 1):
         pl.semaphore_signal(barrier, inc=1, device_id=cdev(k), device_id_type=MESH)
-    for h in range(1, NZ):
+    for h in ALONG:
         pl.semaphore_signal(barrier, inc=1, device_id=zdev(h), device_id_type=MESH)
 
     load_c = [
@@ -135,6 +140,7 @@
         return [(CUR.at[turn], NRM, g, r0, g, True) for r0 in starts for g in groups]
 
     mine_at, theirs_at = range(0, ROWS, RB), range(ROWS, 2 * ROWS, RB)
+    meet()
     for c in load_c:
         c.wait()
     for g in range(2):
@@ -143,6 +149,7 @@
     load_e[0].wait()
     mine, theirs = pl.ds(0, ROWS), pl.ds(ROWS, ROWS)
 
+    late = []
     for turn in range(ITERS):
         last = turn == ITERS - 1
         if turn == 0:
@@ -150,7 +157,7 @@
             for r0 in mine_at:
                 items += own_items(0, range(2), [r0])
                 items += [(CO, NRO, g, r0, 2 + g, False) for g in range(2)]
-            run_scores(items, {2: meet, 4: load_e[1].wait})
+            run_scores(items, {4: load_e[1].wait})
             XS[turn] = lse2([LG[i, :, mine] for i in range(4)])
         else:
             run_scores(own_items(turn, [0], theirs_at), {})
@@ -163,17 +170,16 @@
             XS[turn] = lse2([both, SR[0]])
 
         sends = [
-            remote(XS.at[turn], XR.at[turn, k - 1], x_s.at[turn, k - 1], x_r.at[turn, k - 1], cdev(k))
-            for k in range(1, NC)
+            remote(XS.at[turn], XR.at[turn, k], x_s.at[turn], x_r.at[turn], cdev(k)) for k in range(NC - 1)
         ]
         for c in sends:
             c.start()
         if turn == 0:
-            send_e[0].wait()
-            run_scores(own_items(0, range(2), theirs_at), {2: send_e[1].wait})
-
-        for c in sends:
-            c.wait()
+            send_e[0].wait_recv()
+            run_scores(own_items(0, range(2), theirs_at), {2: send_e[1].wait_recv})
+
+        late.append(remote(XR.at[turn], XR.at[turn], x_s.at[turn], x_r.at[turn], sib))
+        late[-1].wait_recv()
         total = lse2([XS[turn]] + [XR[turn, k] for k in range(NC - 1)])
         SS[turn] = total
         LOC[:, mine] = total
@@ -205,7 +211,7 @@
             weights(r0)
         ring = {
             (w, c, k): remote(
-                RSB.at[turn, i], RRB.at[turn, i], rs_s.at[turn, i], rs_r.at[turn, i], zdev(CHAINS[c][0])
+                RSB.at[turn, i], RRB.at[turn, i], rs_s.at[turn], rs_r.at[turn, i], zdev(CHAINS[c][0])
             )
             for (w, c, k), i in MSG.items()
         }
@@ -231,16 +237,15 @@
             sums(q, pl.ds(0, 2 * ROWS))
         MS[turn] = jnp.sum(MACC[...].T, axis=0, keepdims=True)
         masses = [
-            remote(MS.at[turn], MR.at[turn, h - 1], m_s.at[turn, h - 1], m_r.at[turn, h - 1], zdev(h))
-            for h in range(1, NZ)
+            remote(MS.at[turn], MR.at[turn, h - 1], m_s.at[turn], m_r.at[turn], zdev(h)) for h in ALONG
         ]
         for c in masses:
             c.start()
         for k in range(1, 4):
             for w in range(WAVES):
                 ring_hop(w, k)
-        for c in masses:
-            c.wait()
+        late.append(remote(MR.at[turn], MR.at[turn], m_s.at[turn], m_r.at[turn], sib))
+        late[-1].wait_recv()
         lane = lax.broadcasted_iota(jnp.int32, (CHUNK, 128), 1)
         row = lax.broadcasted_iota(jnp.int32, (CHUNK, 128), 0)
         acc = jnp.zeros((CHUNK, 128), F32)
@@ -265,16 +270,16 @@
             dst = src if last else place(-d * (k + 1), piece)
             if last and k == 0:
                 src = CUR.at[0, pl.ds(piece * PIECE, PIECE)]
-            gather[w, c, k] = remote(src, dst, ag_s.at[turn, i], ag_r.at[turn, i], zdev(d))
+            gather[w, c, k] = remote(src, dst, ag_s.at[turn], ag_r.at[turn, i], zdev(d))
             if last:
                 got = place(-d * (k + 1), 2 * w + h)
-                pairs[w, c, k] = remote(got, got, o_s.at[i], o_r.at[i], sib)
+                pairs[w, c, k] = remote(got, got, o_s.at[0], o_r.at[0], sib)
         if last:
             for w in range(WAVES):
                 start = 2 * w * PIECE
                 fresh = CUR.at[0, pl.ds(start, 2 * PIECE)]
                 rows = out.at[pl.ds(pl.multiple_of(chunk_row(SLOT[0]) + start, 2 * PIECE), 2 * PIECE)]
-                pairs[w] = remote(fresh, rows, o_s.at[NMSG + w], o_r.at[NMSG + w], sib)
+                pairs[w] = remote(fresh, rows, o_s.at[0], o_r.at[0], sib)
                 keeps.append(pltpu.make_async_copy(fresh, rows, o_l.at[w]))
 
         def finish(w):
@@ -327,12 +332,14 @@
             gather_hop(0, 4)
             gather_hop(1, 4)
             store_norms(NRM, CUR.at[turn + 1], 0)
-        for key in MSG:
-            ring[key].wait_send()
-            gather[key].wait_send()
-
-    for c in list(pairs.values()) + keeps:
+        late.append(remote(RSB.at[turn], RSB.at[turn], rs_s.at[turn], rs_r.at[turn, 0], sib))
+        late.append(remote(RSB.at[turn], RSB.at[turn], ag_s.at[turn], ag_r.at[turn, 0], sib))
+
+    for c in late + send_e:
+        c.wait_send()
+    for c in keeps:
         c.wait()
+    remote(CUR.at[1], CUR.at[1], o_s.at[0], o_r.at[0], sib).wait()
 
 
 def per_device(embeds, centroids):
@@ -371,19 +378,19 @@
             dma((NZ + 1,)),
             dma((ROWS // RB,)),
             dma((ROWS // RB,)),
-            dma((ITERS, NC - 1)),
-            dma((ITERS, NC - 1)),
+            dma((ITERS,)),
+            dma((ITERS,)),
             dma((ITERS + 1,)),
             dma((ITERS + 1,)),
-            dma((ITERS, NZ - 1)),
-            dma((ITERS, NZ - 1)),
+            dma((ITERS,)),
+            dma((ITERS,)),
+            dma((ITERS,)),
             dma((ITERS, NMSG)),
-            dma((ITERS, NMSG)),
-            dma((ITERS, NMSG)),
+            dma((ITERS,)),
             dma((ITERS, NMSG)),
             dma((WAVES,)),
-            dma((NMSG + WAVES,)),
-            dma((NMSG + WAVES,)),
+            dma((1,)),
+            dma((1,)),
         ],
         compiler_params=pltpu.CompilerParams(
             collective_id=0, has_side_effects=True, vmem_limit_bytes=50 * 1024 * 1024

time: 94.8 us -> 93.1 us (0.982)
  Pallas kernels: 92.2 us -> 90.5 us
    pallas_call x1, Pallas kernels: 92.2 us -> 90.5 us  [per_device(): pl.pallas_call(kernel, out_shape=(jax.ShapeDtypeStruct((CENTS, D), BF16),...]
where the time goes in v4:
time: 93.1 us
  Pallas kernels  90.5 us (97%)
  local copies, waits for them, and re-layouts  1.92 us (2%)
    pallas_call x1, Pallas kernels, per_device(): pl.pallas_call(kernel, out_shape=(jax.ShapeDtypeStruct((CENTS, D), BF16),...  90.5 us
    unnamed x2, local copies, waits for them, and re-layouts  1.92 us

profile of v4, /device:TPU:1, one launch (start us, length us, event | category | flops | bytes accessed | tf_op | source)
XLA Modules:
  0.0 93.1 jit_solution(4419379827391604507)
XLA Ops:
  0.6 90.5 %shard_map.41 = (bf16[1024,1024]{1,0:T(8,128)(2,1)S(1)}, f32[1536]{0:T(1024)S(1)}) custom-call(bf16[1536,1024]{1,0:T(8,128)(2,1)} %emb.1, bf16[1024,1024]{1,0:T(8,128)(2,1)} %cen.1), custom_call_target="tpu_custom_call" | custom-call | tf_op jit(solution)/shard_map/pallas_call | solution.py:347
  91.1 1.3 %copy.6 = bf16[1024,1024]{1,0:T(8,128)(2,1)} copy(bf16[1024,1024]{1,0:T(8,128)(2,1)S(1)} %get-tuple-element.4) | data formatting | bytes 4194304
  92.5 0.6 copy.7

commit v5 on v4

--- a/solution.py
+++ b/solution.py
@@ -38,6 +38,10 @@
 PEERS = [(dx, dy) for dx in range(NX) for dy in range(NY) if dx or dy]
 PEERS.sort(key=lambda p: -min(p[0], NX - p[0]) - min(p[1], NY - p[1]))
 ALONG = sorted(range(1, NZ), key=lambda h: -min(h, NZ - h))
+LINKS = {4: (1, 2, 1, 1), 3: (1, 1, 1)}
+SUMMED = {4: (4, 3, 1, 2), 3: (3, 2, 1)}
+ADDS = {4: ((), (0,), (1, 3), ()), 3: ((), (0,), (1,))}
+HELD = {4: (0, 1, 3, 1), 3: (0, 1, 2)}
 MESH = pl.DeviceIdType.MESH
 F32 = jnp.float32
 BF16 = jnp.bfloat16
@@ -211,39 +215,40 @@
             weights(r0)
         ring = {
             (w, c, k): remote(
-                RSB.at[turn, i], RRB.at[turn, i], rs_s.at[turn], rs_r.at[turn, i], zdev(CHAINS[c][0])
+                RSB.at[turn, i], RRB.at[turn, i], rs_s.at[turn], rs_r.at[turn, i],
+                zdev(CHAINS[c][0] * LINKS[CHAINS[c][2]][k]),
             )
             for (w, c, k), i in MSG.items()
         }
 
-        def ring_hop(w, k, chains=range(4)):
-            for c, (d, h, hops) in enumerate(CHAINS):
-                if k < hops and c in chains:
-                    o = (d * (hops - k)) % NZ
+        def ring_send(k, chains):
+            for w in range(WAVES):
+                for c in chains:
+                    d, h, reach = CHAINS[c]
+                    o = (d * SUMMED[reach][k]) % NZ
                     v = SUMS[pl.ds(SLOT[o] * CHUNK + (2 * w + h) * PIECE, PIECE), :]
-                    if k:
-                        ring[w, c, k - 1].wait_recv()
-                        v = v + RRB[turn, MSG[w, c, k - 1]].astype(F32)
+                    for j in ADDS[reach][k]:
+                        ring[w, c, j].wait_recv()
+                        v = v + RRB[turn, MSG[w, c, j]].astype(F32)
                     RSB[turn, MSG[w, c, k]] = v.astype(BF16)
                     ring[w, c, k].start()
 
         sums(0, theirs, add=True)
-        for w in range(WAVES):
-            ring_hop(w, 0, (0, 1, 2))
+        ring_send(0, (0, 1, 2))
         sums(1, theirs, add=True)
-        for w in range(WAVES):
-            ring_hop(w, 0, (3,))
-        for q in (2, 3):
-            sums(q, pl.ds(0, 2 * ROWS))
+        ring_send(0, (3,))
+        ring_send(3, (0,))
+        sums(2, pl.ds(0, 2 * ROWS))
+        ring_send(3, (1,))
+        sums(3, pl.ds(0, 2 * ROWS))
         MS[turn] = jnp.sum(MACC[...].T, axis=0, keepdims=True)
         masses = [
             remote(MS.at[turn], MR.at[turn, h - 1], m_s.at[turn], m_r.at[turn], zdev(h)) for h in ALONG
         ]
         for c in masses:
             c.start()
-        for k in range(1, 4):
-            for w in range(WAVES):
-                ring_hop(w, k)
+        for k in (1, 2):
+            ring_send(k, range(4))
         late.append(remote(MR.at[turn], MR.at[turn], m_s.at[turn], m_r.at[turn], sib))
         late[-1].wait_recv()
         lane = lax.broadcasted_iota(jnp.int32, (CHUNK, 128), 1)
@@ -264,15 +269,16 @@
 
         gather, pairs, keeps = {}, {}, []
         for (w, c, k), i in MSG.items():
-            d, h, hops = CHAINS[c]
+            d, h, reach = CHAINS[c]
             piece = 2 * w + h
-            src = place(-d * k, piece)
-            dst = src if last else place(-d * (k + 1), piece)
+            held, links = HELD[reach][k], LINKS[reach][k]
+            src = place(-d * held, piece)
+            dst = src if last else place(-d * (held + links), piece)
             if last and k == 0:
                 src = CUR.at[0, pl.ds(piece * PIECE, PIECE)]
-            gather[w, c, k] = remote(src, dst, ag_s.at[turn], ag_r.at[turn, i], zdev(d))
+            gather[w, c, k] = remote(src, dst, ag_s.at[turn], ag_r.at[turn, i], zdev(d * links))
             if last:
-                got = place(-d * (k + 1), 2 * w + h)
+                got = place(-d * (held + links), piece)
                 pairs[w, c, k] = remote(got, got, o_s.at[0], o_r.at[0], sib)
         if last:
             for w in range(WAVES):
@@ -289,9 +295,8 @@
                 v = SUMS[rows, :] + CUR[turn, rows, :].astype(F32)
                 for c in range(4):
                     if CHAINS[c][1] == h:
-                        k = CHAINS[c][2] - 1
-                        ring[w, c, k].wait_recv()
-                        v = v + RRB[turn, MSG[w, c, k]].astype(F32)
+                        ring[w, c, 2].wait_recv()
+                        v = v + RRB[turn, MSG[w, c, 2]].astype(F32)
                 fresh = (v * inv[piece * PIECE : (piece + 1) * PIECE]).astype(BF16)
                 if last:
                     CUR[0, pl.ds(piece * PIECE, PIECE), :] = fresh
@@ -304,33 +309,35 @@
                 pairs[w].start()
                 keeps[w].start()
 
-        def gather_hop(w, k):
-            for c, (d, h, hops) in enumerate(CHAINS):
-                if k <= hops:
-                    gather[w, c, k - 1].wait_recv()
-                    if k < hops:
-                        gather[w, c, k].start()
+        def gather_stage(stage):
+            for w in range(WAVES):
+                for c, (d, h, reach) in enumerate(CHAINS):
+                    gather[w, c, stage - 1].wait_recv()
+                    if stage < 3:
+                        gather[w, c, stage].start()
+                    if stage == 1 and reach == 4:
+                        gather[w, c, 3].start()
                     if last:
-                        pairs[w, c, k - 1].start()
+                        pairs[w, c, stage - 1].start()
+            if stage == 2:
+                for w in range(WAVES):
+                    for c in (0, 1):
+                        gather[w, c, 3].wait_recv()
+                        if last:
+                            pairs[w, c, 3].start()
 
         for w in range(WAVES):
             finish(w)
-        for k in (1, 2):
-            for w in range(WAVES):
-                gather_hop(w, k)
+        gather_stage(1)
+        gather_stage(2)
         if last:
-            for k in (3, 4):
-                for w in range(WAVES):
-                    gather_hop(w, k)
+            gather_stage(3)
             row_lse[...] = (SS[turn] * LN2).reshape(ROWS)
         else:
             store_norms(NRM, CUR.at[turn + 1], 1)
             run_scores(own_items(turn + 1, [1], mine_at), {})
-            gather_hop(0, 3)
-            gather_hop(1, 3)
             run_scores(own_items(turn + 1, [1], theirs_at), {})
-            gather_hop(0, 4)
-            gather_hop(1, 4)
+            gather_stage(3)
             store_norms(NRM, CUR.at[turn + 1], 0)
         late.append(remote(RSB.at[turn], RSB.at[turn], rs_s.at[turn], rs_r.at[turn, 0], sib))
         late.append(remote(RSB.at[turn], RSB.at[turn], ag_s.at[turn], ag_r.at[turn, 0], sib))

time: 93.1 us -> 93.1 us (level)
  no operation moved by 1% of the time
where the time goes in v5:
time: 93.1 us; the launch traced here: 93 us
  Pallas kernels  90.5 us (97%)
  local copies, waits for them, and re-layouts  1.92 us (2%)
    pallas_call x1, Pallas kernels, per_device(): pl.pallas_call(kernel, out_shape=(jax.ShapeDtypeStruct((CENTS, D), BF16),...  90.5 us
    unnamed x2, local copies, waits for them, and re-layouts  1.92 us

profile of v5, /device:TPU:1, one launch (start us, length us, event | category | flops | bytes accessed | tf_op | source)
XLA Modules:
  0.0 93.0 jit_solution(17483997737170713585)
XLA Ops:
  0.6 90.5 %shard_map.41 = (bf16[1024,1024]{1,0:T(8,128)(2,1)S(1)}, f32[1536]{0:T(1024)S(1)}) custom-call(bf16[1536,1024]{1,0:T(8,128)(2,1)} %emb.1, bf16[1024,1024]{1,0:T(8,128)(2,1)} %cen.1), custom_call_target="tpu_custom_call" | custom-call | tf_op jit(solution)/shard_map/pallas_call | solution.py:354
  91.1 1.3 %copy.6 = bf16[1024,1024]{1,0:T(8,128)(2,1)} copy(bf16[1024,1024]{1,0:T(8,128)(2,1)S(1)} %get-tuple-element.4) | data formatting | bytes 4194304
  92.4 0.6 copy.7

commit v6 on v5

--- a/solution.py
+++ b/solution.py
@@ -99,21 +99,18 @@
     load_e = [
         pltpu.make_async_copy(emb.at[pl.ds(b * RB, RB)], E.at[pl.ds(b * RB, RB)], ld_e.at[b]) for b in range(NB)
     ]
-    for c in load_c[:NZ]:
-        c.start()
-    load_e[0].start()
-    load_c[NZ].start()
-    for c in load_e[1:]:
+    for c in load_e + load_c:
         c.start()
     send_e = [
-        remote(emb.at[pl.ds(b * RB, RB)], E.at[pl.ds(ROWS + b * RB, RB)], es_s.at[b], es_r.at[b], sib)
+        remote(E.at[pl.ds(b * RB, RB)], E.at[pl.ds(ROWS + b * RB, RB)], es_s.at[b], es_r.at[b], sib)
         for b in range(NB)
     ]
 
     def meet():
         pl.semaphore_wait(barrier, NC - 1 + NZ - 1 + 1)
-        for c in send_e:
-            c.start()
+        for load, send in zip(load_e, send_e):
+            load.wait()
+            send.start()
 
     def store_norms(dst, src, g):
         rows = pl.ds(g * GROUP, GROUP)
@@ -150,7 +147,6 @@
     for g in range(2):
         store_norms(NRM, CUR.at[0], g)
         store_norms(NRO, CO, g)
-    load_e[0].wait()
     mine, theirs = pl.ds(0, ROWS), pl.ds(ROWS, ROWS)
 
     late = []
@@ -161,7 +157,7 @@
             for r0 in mine_at:
                 items += own_items(0, range(2), [r0])
                 items += [(CO, NRO, g, r0, 2 + g, False) for g in range(2)]
-            run_scores(items, {4: load_e[1].wait})
+            run_scores(items, {})
             XS[turn] = lse2([LG[i, :, mine] for i in range(4)])
         else:
             run_scores(own_items(turn, [0], theirs_at), {})

time: 93.1 us -> 92.5 us (level)
  no operation moved by 1% of the time
where the time goes in v6:
time: 92.5 us; the launch traced here: 92.4 us
  Pallas kernels  89.9 us (97%)
  local copies, waits for them, and re-layouts  1.92 us (2%)
    pallas_call x1, Pallas kernels, per_device(): pl.pallas_call(kernel, out_shape=(jax.ShapeDtypeStruct((CENTS, D), BF16),...  89.9 us
    unnamed x2, local copies, waits for them, and re-layouts  1.92 us

profile of v6, /device:TPU:1, one launch (start us, length us, event | category | flops | bytes accessed | tf_op | source)
XLA Modules:
  0.0 92.4 jit_solution(12577302317580886658)
XLA Ops:
  0.6 89.9 %shard_map.41 = (bf16[1024,1024]{1,0:T(8,128)(2,1)S(1)}, f32[1536]{0:T(1024)S(1)}) custom-call(bf16[1536,1024]{1,0:T(8,128)(2,1)} %emb.1, bf16[1024,1024]{1,0:T(8,128)(2,1)} %cen.1), custom_call_target="tpu_custom_call" | custom-call | tf_op jit(solution)/shard_map/pallas_call | solution.py:350
  90.5 1.3 %copy.6 = bf16[1024,1024]{1,0:T(8,128)(2,1)} copy(bf16[1024,1024]{1,0:T(8,128)(2,1)S(1)} %get-tuple-element.4) | data formatting | bytes 4194304
  91.8 0.6 copy.7
